TPU v7x, 32 devices: a whole 2x2x4 slice. The times are simulated.
32 devices in a mesh: gas: 8 (over z, y), space: 4 (over x, core).
Axes of the slice: x: 2, y: 2, z: 4, core: 2. Of those that a mesh axis runs over, the one named last changes fastest.
Arguments:
- particle_amount: bfloat16 [1024, 256, 8, 128], P('gas', 'space'), may hold values from 0 to 1
- section_opacity: bfloat16 [1024, 16], P('gas'), may hold values from 0.0009994507 to 0.0099487305
- species_opacity_factor: float32 [16], replicated, may hold values from 0.05 to 0.5
- absorber_molefraction: float32 [256, 8, 128], P('space'), may hold values from 0 to 1
- scaled_heat_level: float32 [256, 8, 128], P('space'), may hold values from 0.24 to 1.68
- wall_touching_flag: int32 [256, 8, 128], P('space'), may hold values 0 or 1
- fraction_polynomial: float32 [16, 3], replicated, may hold values from 0.05 to 1.35
Outputs:
- divergence: float32 [256, 8, 128], P('space')
- average_radiative_loss: float32 [], replicated
All inputs are finite; a program needn't handle non-finite values. No bound on the sum of `wall_touching_flag` on one device may be relied on, other than what follows from the above.
Results may differ from a plain program's by a relative error of at most 0.0003.
Values sent between devices are 32-bit elements; how exact they have to be, the bound alone decides.
A program may use at most 64 MiB of HBM per device.

v0:
```python
import jax
import jax.numpy as jnp
from jax import lax
from jax.sharding import PartitionSpec as P

SWEEPS = 6


KAPPA_FLOOR = 0.5
WALL_LOSS = 0.5
LAM_LOW = 0.5
LAM_HIGH = 12.0


def with_halo(x, sides, width):
    for axis, dim in sides:
        peers, length = (lax.axis_size(axis), x.shape[dim])
        up = [(i, (i + 1) % peers) for i in range(peers - 1)]
        down = [(j, i) for i, j in up]
        last = lax.slice_in_dim(x, length - width, length, axis=dim)
        leading = lax.slice_in_dim(x, 0, width, axis=dim)
        before = lax.ppermute(last, axis, up)
        after = lax.ppermute(leading, axis, down)
        x = jnp.concatenate([before, x, after], axis=dim)
    return x


def lower(values, dimension):
    border = jnp.zeros_like(lax.slice_in_dim(values, 0, 1, axis=dimension))
    return jnp.concatenate(
        [border, lax.slice_in_dim(values, 0, values.shape[dimension] - 1, axis=dimension)],
        dimension,
    )


def upper(values, dimension):
    border = jnp.zeros_like(lax.slice_in_dim(values, 0, 1, axis=dimension))
    return jnp.concatenate(
        [lax.slice_in_dim(values, 1, values.shape[dimension], axis=dimension), border], dimension
    )


def coupling(paired_total):
    positive = paired_total > 0.0
    return jnp.where(positive, 2.0 / (3.0 * jnp.where(positive, paired_total, 1.0)), 0.0)


def per_device(
    particle_amount,
    section_opacity,
    species_opacity_factor,
    absorber_molefraction,
    scaled_heat_level,
    wall_touching_flag,
    fraction_polynomial,
):
    gas_count = lax.axis_size("gas")
    per_gas = species_opacity_factor.shape[0] // gas_count
    first_gas = lax.axis_index("gas") * per_gas
    width_x = absorber_molefraction.shape[0]
    total_x = width_x * lax.axis_size("space")
    soot_flat = particle_amount.reshape(particle_amount.shape[0], -1)
    summed_all = lax.psum(
        lax.dot_general(
            section_opacity, soot_flat, (((0,), (0,)), ((), ())), preferred_element_type=jnp.float32
        ),
        "gas",
    )
    own_soot = lax.dynamic_slice_in_dim(summed_all, first_gas, per_gas, 0)
    own_soot = own_soot.reshape((per_gas,) + absorber_molefraction.shape)
    strength = lax.dynamic_slice_in_dim(species_opacity_factor, first_gas, per_gas, 0)
    component_lines = lax.dynamic_slice_in_dim(fraction_polynomial, first_gas, per_gas, 0)
    absorption = (
        KAPPA_FLOOR + strength[:, None, None, None] * absorber_molefraction[None] + own_soot
    )
    heat_level_square = scaled_heat_level * scaled_heat_level
    component_fractions = (
        component_lines[:, 0][:, None, None, None]
        + component_lines[:, 1][:, None, None, None] * scaled_heat_level[None]
        + component_lines[:, 2][:, None, None, None] * heat_level_square[None]
    )
    emitted_power = component_fractions * (heat_level_square * heat_level_square)[None]
    base_diag = absorption + WALL_LOSS * wall_touching_flag.astype(jnp.float32)[None]
    halo_depth = 1
    widened = with_halo(jnp.stack([absorption, base_diag]), (("space", 2),), halo_depth)
    wide_abs = widened[0]
    inner_abs = wide_abs[:, 1:-1]
    couple = (
        coupling(inner_abs + wide_abs[:, :-2]),
        coupling(inner_abs + wide_abs[:, 2:]),
        coupling(inner_abs + lower(inner_abs, 2)),
        coupling(inner_abs + upper(inner_abs, 2)),
        coupling(inner_abs + lower(inner_abs, 3)),
        coupling(inner_abs + upper(inner_abs, 3)),
    )
    diagonal = widened[1][:, 1:-1]
    for weight_face in couple:
        diagonal = diagonal + weight_face
    rows_wide = width_x + 2 * halo_depth - 2
    global_row = (
        lax.axis_index("space") * width_x - halo_depth + 1 + jnp.arange(rows_wide, dtype=jnp.int32)
    )
    inside = ((global_row >= 0) & (global_row < total_x)).astype(jnp.float32)[None, :, None, None]
    centre = (LAM_HIGH + LAM_LOW) / 2.0
    spread_half = (LAM_HIGH - LAM_LOW) / 2.0
    ratio_sigma = centre / spread_half
    residual = absorption * emitted_power
    direction = residual / centre
    iterate = jnp.zeros_like(residual)
    ratio_now = 1.0 / ratio_sigma
    for sweep_index in range(SWEEPS):
        residual, direction = (residual, with_halo(direction, (("space", 1),), 1))
        span_rows = direction.shape[1]
        middle = direction[:, 1:-1]
        applied = diagonal * middle
        beside = (
            direction[:, :-2],
            direction[:, 2:],
            lower(middle, 2),
            upper(middle, 2),
            lower(middle, 3),
            upper(middle, 3),
        )
        for weight_face, neighbour in zip(couple, beside):
            applied = applied - weight_face * neighbour
        inner_start = (span_rows - width_x) // 2
        iterate = iterate + direction[:, inner_start : inner_start + width_x]
        residual = (residual - applied) * inside
        ratio_next = 1.0 / (2.0 * ratio_sigma - ratio_now)
        direction = (
            ratio_next * ratio_now * middle + 2.0 * ratio_next / spread_half * residual
        ) * inside
        ratio_now = ratio_next
    gas_terms = absorption * (emitted_power - iterate)
    divergence = lax.psum(jnp.sum(gas_terms, axis=0), "gas")
    cell_count = total_x * absorber_molefraction.shape[1] * absorber_molefraction.shape[2]
    average_radiative_loss = lax.psum(jnp.sum(divergence), "space") / cell_count
    return (divergence, average_radiative_loss)


def solution(mesh):
    return jax.shard_map(
        per_device,
        mesh=mesh,
        in_specs=(
            P("gas", "space", None, None),
            P("gas", None),
            P(),
            P("space", None, None),
            P("space", None, None),
            P("space", None, None),
            P(),
        ),
        out_specs=(P("space", None, None), P()),
        check_vma=False,
    )
```

profile of v0, /device:TPU:0, one launch (start us, length us, event | category | flops | bytes accessed | tf_op | source)
XLA Modules:
  0.0 324.8 jit_solution(6322552649570124776)
XLA Ops:
  7.2 0.0 copy-start
  7.2 0.0 all-reduce.27.cloned.1.call-start
  7.2 0.6 copy-done
  7.9 16.8 %fusion = f32[16,65536]{1,0:T(8,128)} fusion(bf16[128,16]{0,1:T(8,128)(2,1)S(1)} %copy-done, bf16[16,8,512,128]{3,2,1,0:T(8,128)(2,1)} %bitcast.31), kind=kOutput, calls=%fused_computation | convolution fusion | flops 268435456 | bytes 20975616 | tf_op jit(solution)/shard_map/dot_general | solution.py:64
  24.6 0.0 copy-start.2
  24.7 0.0 all-reduce.27.cloned.1.call-update
  24.7 0.0 all-reduce.29.cloned.1.call-start
  24.7 0.6 copy-done.5
  25.3 0.1 dynamic_slice.9
  25.4 0.1 constant_dynamic-slice_fusion
  25.4 0.2 copy-done.3
  25.6 0.1 copy-done.1
  25.7 158.1 %all-reduce.27.cloned.1.call-done = f32[16,65536]{1,0:T(8,128)} async-done(((f32[16,65536]{1,0:T(8,128)}), f32[16,65536]{1,0:T(8,128)}) %all-reduce.27.cloned.1.call-update) | async-done | bytes 4194320 | tf_op jit(solution)/shard_map/psum | solution.py:63
  183.8 1.8 dynamic-slice_bitcast_fusion
  185.6 0.3 broadcast_multiply_fusion
  185.9 0.2 fusion.97
  186.1 0.1 fusion.96
  186.1 0.2 broadcast_add_fusion
  186.3 1.7 collective-permute-start
  188.0 1.3 collective-permute-start.1
  189.3 4.3 %collective-permute-start.2 = (f32[2,1,8,128]{3,2,1,0:T(8,128)S(1)}, f32[2,1,8,128]{3,2,1,0:T(8,128)S(1)}, u32[]{:S(2)}, u32[]{:S(2)}) collective-permute-start(f32[2,1,8,128]{3,2,1,0:T(8,128)S(1)} %get-tuple-element.47), channel_id=1, source_target_pairs={{0,1},{1,2},{2,3},{4,5},{5,6},{6,7},{8,9},{9,10},{10,11},{12,13},{... | collective-permute-start | bytes 24584 | tf_op jit(solution)/shard_map/ppermute | solution.py:22
  193.7 1.5 collective-permute-start.3
  195.2 0.0 collective-permute-done
  195.2 0.0 collective-permute-done.1
  195.2 0.1 pad_maximum_fusion
  195.3 0.1 slice_bitcast_fusion
  195.3 0.2 fusion.81
  195.5 0.1 fusion.82
  195.6 0.0 collective-permute-done.2
  195.6 2.4 collective-permute-done.3
  198.0 1.6 add_multiply_fusion.3
  199.6 0.2 fusion.94
  199.8 4.3 %collective-permute-start.4 = (f32[2,1,8,128]{3,2,1,0:T(8,128)S(1)}, f32[2,1,8,128]{3,2,1,0:T(8,128)S(1)}, u32[]{:S(2)}, u32[]{:S(2)}) collective-permute-start(f32[2,1,8,128]{3,2,1,0:T(8,128)S(1)} %get-tuple-element.41), channel_id=1, source_target_pairs={{0,1},{1,2},{2,3},{4,5},{5,6},{6,7},{8,9},{9,10},{10,11},{12,13},{... | collective-permute-start | bytes 24584 | tf_op jit(solution)/shard_map/ppermute | solution.py:22
  204.1 1.3 collective-permute-start.5
  205.4 0.1 fusion.93
  205.5 0.0 collective-permute-done.4
  205.5 1.7 collective-permute-done.5
  207.2 0.6 add_multiply_fusion.2
  207.8 0.2 fusion.91
  208.0 3.8 %collective-permute-start.6 = (f32[2,1,8,128]{3,2,1,0:T(8,128)S(1)}, f32[2,1,8,128]{3,2,1,0:T(8,128)S(1)}, u32[]{:S(2)}, u32[]{:S(2)}) collective-permute-start(f32[2,1,8,128]{3,2,1,0:T(8,128)S(1)} %get-tuple-element.35), channel_id=1, source_target_pairs={{0,1},{1,2},{2,3},{4,5},{5,6},{6,7},{8,9},{9,10},{10,11},{12,13},{... | collective-permute-start | bytes 24584 | tf_op jit(solution)/shard_map/ppermute | solution.py:22
  211.8 1.3 collective-permute-start.7
  213.2 0.1 fusion.90
  213.2 0.0 collective-permute-done.6
  213.2 1.7 collective-permute-done.7
  214.9 1.0 add_multiply_fusion.1
  216.0 0.2 fusion.88
  216.2 3.8 %collective-permute-start.8 = (f32[2,1,8,128]{3,2,1,0:T(8,128)S(1)}, f32[2,1,8,128]{3,2,1,0:T(8,128)S(1)}, u32[]{:S(2)}, u32[]{:S(2)}) collective-permute-start(f32[2,1,8,128]{3,2,1,0:T(8,128)S(1)} %get-tuple-element.29), channel_id=1, source_target_pairs={{0,1},{1,2},{2,3},{4,5},{5,6},{6,7},{8,9},{9,10},{10,11},{12,13},{... | collective-permute-start | bytes 24584 | tf_op jit(solution)/shard_map/ppermute | solution.py:22
  220.0 1.3 collective-permute-start.9
  221.3 0.1 fusion.87
  221.4 0.0 collective-permute-done.8
  221.4 1.7 collective-permute-done.9
  223.1 2.1 add_multiply_fusion
  225.2 0.2 fusion.85
  225.4 3.8 %collective-permute-start.10 = (f32[2,1,8,128]{3,2,1,0:T(8,128)S(1)}, f32[2,1,8,128]{3,2,1,0:T(8,128)S(1)}, u32[]{:S(2)}, u32[]{:S(2)}) collective-permute-start(f32[2,1,8,128]{3,2,1,0:T(8,128)S(1)} %get-tuple-element.23), channel_id=1, source_target_pairs={{0,1},{1,2},{2,3},{4,5},{5,6},{6,7},{8,9},{9,10},{10,11},{12,13},{... | collective-permute-start | bytes 24584 | tf_op jit(solution)/shard_map/ppermute | solution.py:22
  229.2 1.3 collective-permute-start.11
  230.5 0.1 fusion.84
  230.6 0.0 collective-permute-done.10
  230.6 1.7 collective-permute-done.11
  232.3 3.9 %fusion.77 = f32[64,8,128]{2,1,0:T(8,128)} fusion(f32[2,64,8,128]{3,2,1,0:T(8,128)S(1)} %get-tuple-element.10, f32[2,64,8,127]{3,2,1,0:T(8,128)S(1)} %get-tuple-element.28, f32[2,64,8,128]{3,2,1,0:T(8,128)S(1)} %get-tuple-element.7, f32[2,64,8,127]{3,2,1,0:T(8,128)S(1)} %get-tuple-element.27, f32[2,64,8,128]{3,2,1,0:T(8,128)S(1)} %get-tuple-element.6, ...), kind=kLoop, calls=%fused_computation.113 | loop fusion | flops 13172736 | bytes 16548128 | tf_op jit(solution)/shard_map/reduce_sum | solution.py:135
  236.2 0.0 all-reduce.29.cloned.1.call-update
  236.2 70.4 %all-reduce.29.cloned.1.call-done = f32[64,8,128]{2,1,0:T(8,128)} async-done(((f32[64,8,128]{2,1,0:T(8,128)}), f32[64,8,128]{2,1,0:T(8,128)}) %all-reduce.29.cloned.1.call-update) | async-done | bytes 262160 | tf_op jit(solution)/shard_map/psum | solution.py:135
  306.6 1.6 reduce_sum.19
  308.2 6.3 %psum.23 = f32[]{:T(128)} all-reduce(f32[]{:T(128)} %reduce_sum.19), channel_id=1, replica_groups=mesh['gas'=8,'space'=4] {'space'}, use_global_device_ids=true, to_apply=%region_4.5 | all-reduce | flops 1 | bytes 8 | tf_op jit(solution)/shard_map/psum | solution.py:137
  315.2 1.7 copy.26
  (16 shorter events, 0.1 us)
Async XLA Ops:
  7.2 0.7 copy-start
  7.2 176.6 %all-reduce.27.cloned.1.call-start = ((), (), s32[]{:S(2)}) async-start(), calls=%async_computation | async-start | bytes 8388608 | tf_op jit(solution)/shard_map/psum | solution.py:63
  24.6 0.7 copy-start.5
  24.6 0.7 copy-start.4
  24.6 1.0 copy-start.3
  24.6 1.1 copy-start.1
  24.6 160.9 %copy-start.2 = (f32[64,8,128]{2,1,0:T(8,128)S(1)}, f32[64,8,128]{2,1,0:T(8,128)}, u32[]{:S(2)}) copy-start(f32[64,8,128]{2,1,0:T(8,128)} %param.10) | copy-start | bytes 786436
  24.7 281.9 %all-reduce.29.cloned.1.call-start = ((), (), s32[]{:S(2)}) async-start(), calls=%async_computation.1 | async-start | bytes 524288 | tf_op jit(solution)/shard_map/psum | solution.py:135
  186.3 8.8 %collective-permute-start = (f32[2,2,1,8,128]{4,3,2,1,0:T(8,128)S(1)}, f32[2,2,1,8,128]{4,3,2,1,0:T(8,128)S(1)}, u32[]{:S(2)}, u32[]{:S(2)}) collective-permute-start(f32[2,2,1,8,128]{4,3,2,1,0:T(8,128)S(1)} %get-tuple-element.17), channel_id=1, source_target_pairs={{0,1},{1,2},{2,3},{4,5},{5,6},{6,7},{8,9},{9,10},{10,11},{12,13},{... | collective-permute-start | bytes 49160 | tf_op jit(solution)/shard_map/ppermute | solution.py:22
  188.0 7.1 %collective-permute-start.1 = (f32[2,2,1,8,128]{4,3,2,1,0:T(8,128)S(1)}, f32[2,2,1,8,128]{4,3,2,1,0:T(8,128)S(1)}, u32[]{:S(2)}, u32[]{:S(2)}) collective-permute-start(f32[2,2,1,8,128]{4,3,2,1,0:T(8,128)S(1)} %get-tuple-element.18), channel_id=1, source_target_pairs={{1,0},{2,1},{3,2},{5,4},{6,5},{7,6},{9,8},{10,9},{11,10},{13,12},{... | collective-permute-start | bytes 49160 | tf_op jit(solution)/shard_map/ppermute | solution.py:23
  189.3 6.3 %collective-permute-start.2 = (f32[2,1,8,128]{3,2,1,0:T(8,128)S(1)}, f32[2,1,8,128]{3,2,1,0:T(8,128)S(1)}, u32[]{:S(2)}, u32[]{:S(2)}) collective-permute-start(f32[2,1,8,128]{3,2,1,0:T(8,128)S(1)} %get-tuple-element.47), channel_id=1, source_target_pairs={{0,1},{1,2},{2,3},{4,5},{5,6},{6,7},{8,9},{9,10},{10,11},{12,13},{... | collective-permute-start | bytes 24584 | tf_op jit(solution)/shard_map/ppermute | solution.py:22
  193.7 4.3 %collective-permute-start.3 = (f32[2,1,8,128]{3,2,1,0:T(8,128)S(1)}, f32[2,1,8,128]{3,2,1,0:T(8,128)S(1)}, u32[]{:S(2)}, u32[]{:S(2)}) collective-permute-start(f32[2,1,8,128]{3,2,1,0:T(8,128)S(1)} %get-tuple-element.48), channel_id=1, source_target_pairs={{1,0},{2,1},{3,2},{5,4},{6,5},{7,6},{9,8},{10,9},{11,10},{13,12},{... | collective-permute-start | bytes 24584 | tf_op jit(solution)/shard_map/ppermute | solution.py:23
  199.8 5.7 %collective-permute-start.4 = (f32[2,1,8,128]{3,2,1,0:T(8,128)S(1)}, f32[2,1,8,128]{3,2,1,0:T(8,128)S(1)}, u32[]{:S(2)}, u32[]{:S(2)}) collective-permute-start(f32[2,1,8,128]{3,2,1,0:T(8,128)S(1)} %get-tuple-element.41), channel_id=1, source_target_pairs={{0,1},{1,2},{2,3},{4,5},{5,6},{6,7},{8,9},{9,10},{10,11},{12,13},{... | collective-permute-start | bytes 24584 | tf_op jit(solution)/shard_map/ppermute | solution.py:22
  204.1 3.1 collective-permute-start.5
  208.0 5.2 %collective-permute-start.6 = (f32[2,1,8,128]{3,2,1,0:T(8,128)S(1)}, f32[2,1,8,128]{3,2,1,0:T(8,128)S(1)}, u32[]{:S(2)}, u32[]{:S(2)}) collective-permute-start(f32[2,1,8,128]{3,2,1,0:T(8,128)S(1)} %get-tuple-element.35), channel_id=1, source_target_pairs={{0,1},{1,2},{2,3},{4,5},{5,6},{6,7},{8,9},{9,10},{10,11},{12,13},{... | collective-permute-start | bytes 24584 | tf_op jit(solution)/shard_map/ppermute | solution.py:22
  211.8 3.1 collective-permute-start.7
  216.2 5.2 %collective-permute-start.8 = (f32[2,1,8,128]{3,2,1,0:T(8,128)S(1)}, f32[2,1,8,128]{3,2,1,0:T(8,128)S(1)}, u32[]{:S(2)}, u32[]{:S(2)}) collective-permute-start(f32[2,1,8,128]{3,2,1,0:T(8,128)S(1)} %get-tuple-element.29), channel_id=1, source_target_pairs={{0,1},{1,2},{2,3},{4,5},{5,6},{6,7},{8,9},{9,10},{10,11},{12,13},{... | collective-permute-start | bytes 24584 | tf_op jit(solution)/shard_map/ppermute | solution.py:22
  220.0 3.1 collective-permute-start.9
  225.4 5.2 %collective-permute-start.10 = (f32[2,1,8,128]{3,2,1,0:T(8,128)S(1)}, f32[2,1,8,128]{3,2,1,0:T(8,128)S(1)}, u32[]{:S(2)}, u32[]{:S(2)}) collective-permute-start(f32[2,1,8,128]{3,2,1,0:T(8,128)S(1)} %get-tuple-element.23), channel_id=1, source_target_pairs={{0,1},{1,2},{2,3},{4,5},{5,6},{6,7},{8,9},{9,10},{10,11},{12,13},{... | collective-permute-start | bytes 24584 | tf_op jit(solution)/shard_map/ppermute | solution.py:22
  229.2 3.1 collective-permute-start.11
Sparse Core Ops, SparseCore 0:
  24.8 158.9 all-reduce.26
  236.3 70.2 all-reduce.28
where the time goes:
time: 325 us
  waiting for transfers between devices  238 us (73%)
  starting transfers between devices  29.9 us (9%)
  matrix products  16.8 us (5%)
  between operations  16.2 us (5%)
  other arithmetic  11.4 us (4%)
  local copies, waits for them, and re-layouts  6.74 us (2%)
  blocking collectives  6.27 us (2%)
    psum x1, waiting for transfers between devices, per_device(): lax.psum(lax.dot_general(section_opacity, soot_flat, (((0,), (0,)), ((),...  158 us
    psum x1, waiting for transfers between devices, per_device(): divergence = lax.psum(jnp.sum(gas_terms, axis=0), 'gas')  70.4 us
    ppermute x6, starting transfers between devices, with_halo(): before = lax.ppermute(last, axis, up)  21.9 us
    dot_general x1, matrix products, per_device(): lax.dot_general(section_opacity, soot_flat, (((0,), (0,)), ((), ())), pre...  16.8 us
    ppermute x6, waiting for transfers between devices, with_halo(): after = lax.ppermute(leading, axis, down)  9.07 us
    ppermute x6, starting transfers between devices, with_halo(): after = lax.ppermute(leading, axis, down)  7.93 us
  transfers between devices with their start and end apart: 14, of which 7 were waited for; matrix products, arithmetic and copies ran while one was open for 0% of the time, Pallas kernels for 0%

commit v1 on v0

v1 whole, which is shorter than its diff:
```python
import functools

import jax
import jax.numpy as jnp
from jax import lax
from jax.experimental import pallas as pl
from jax.experimental.pallas import tpu as pltpu
from jax.sharding import PartitionSpec as P

SWEEPS = 6
HALO = SWEEPS - 1
KAPPA_FLOOR = 0.5
WALL_LOSS = 0.5
LAM_LOW = 0.5
LAM_HIGH = 12.0
CENTRE = (LAM_HIGH + LAM_LOW) / 2.0
SPREAD = (LAM_HIGH - LAM_LOW) / 2.0
MESH = pl.DeviceIdType.MESH


def reversed_bits(index, bits):
    return sum(((index >> b) & 1) << (bits - 1 - b) for b in range(bits))


def coupling(total):
    positive = total > 0.0
    return jnp.where(positive, 2.0 / (3.0 * jnp.where(positive, total, 1.0)), 0.0)


def kernel(
    n, spaces, slabs, cells,
    kron, amount, strength, mole, heat, flag, poly,
    out, average,
    amount_v, acc, recvs, absorb, heat_w, wall_w, cx, cy, cz, diag, res, rem, dirs,
    parts, totals, mine,
    load_sem, rs_send, rs_recv, halo_send, halo_recv, sum_send, sum_recv,
    gather_send, gather_recv, total_send, total_recv,
):
    bits = n.bit_length() - 1
    me, place = lax.axis_index("gas"), lax.axis_index("space")
    per_gas = acc.shape[2]
    x_rows, rows = heat.shape[0], heat_w.shape[0]
    slab_rows = x_rows // slabs
    order = [0, slabs - 1] + list(range(1, slabs - 1))

    def load(slab):
        return pltpu.make_async_copy(
            amount.at[:, pl.ds(slab * slab_rows, slab_rows)], amount_v.at[slab], load_sem.at[slab]
        )

    for slab in order:
        load(slab).start()

    barrier = pltpu.get_barrier_semaphore()
    for k in range(1, n):
        pl.semaphore_signal(
            barrier, inc=1, device_id={"gas": lax.rem(me + k, n)}, device_id_type=MESH
        )
    for k in range(1, spaces):
        pl.semaphore_signal(
            barrier, inc=1, device_id={"space": lax.rem(place + k, spaces)}, device_id_type=MESH
        )
    heat_w[HALO : HALO + x_rows] = heat[...]
    wall_w[HALO : HALO + x_rows] = WALL_LOSS * flag[...].astype(jnp.float32)
    pl.semaphore_wait(barrier, n - 1 + spaces - 1)

    right, left = lax.rem(place + 1, spaces), lax.rem(place + spaces - 1, spaces)

    def halo_pair(which, before, after, to_right, to_left):
        return [
            pltpu.make_async_remote_copy(
                src_ref=to_right, dst_ref=before,
                send_sem=halo_send.at[which, 0], recv_sem=halo_recv.at[which, 0],
                device_id={"space": right}, device_id_type=MESH,
            ),
            pltpu.make_async_remote_copy(
                src_ref=to_left, dst_ref=after,
                send_sem=halo_send.at[which, 1], recv_sem=halo_recv.at[which, 1],
                device_id={"space": left}, device_id_type=MESH,
            ),
        ]

    pairs = []
    for which, ref in enumerate((heat_w, wall_w)):
        pairs += halo_pair(
            which,
            ref.at[pl.ds(0, HALO)], ref.at[pl.ds(HALO + x_rows, HALO)],
            ref.at[pl.ds(x_rows, HALO)], ref.at[pl.ds(HALO, HALO)],
        )
    for copy in pairs:
        copy.start()

    bases, size = [jnp.int32(0)], n
    for stage in range(bits):
        size //= 2
        bases.append(bases[-1] + ((me >> stage) & 1) * size)
    position = bases[bits]

    def exchange(stage, slab):
        half = n >> (stage + 1)
        bit = (me >> stage) & 1
        partner = me + (1 - 2 * bit) * (1 << stage)
        return pltpu.make_async_remote_copy(
            src_ref=acc.at[slab, pl.ds(bases[stage] + (1 - bit) * half, half)],
            dst_ref=recvs[stage].at[slab],
            send_sem=rs_send.at[stage, slab], recv_sem=rs_recv.at[stage, slab],
            device_id={"gas": partner}, device_id_type=MESH,
        )

    def opacity(slab):
        load(slab).wait()

        def one(x, carry):
            block = amount_v[slab, :, x].reshape(-1, cells)
            value = jnp.dot(kron[...], block, preferred_element_type=jnp.float32)
            acc[slab, :, :, x] = value.reshape((n, per_gas) + acc.shape[4:])
            return carry

        lax.fori_loop(0, slab_rows, one, 0)

    absorb_pair = halo_pair(
        2,
        absorb.at[:, pl.ds(0, HALO)], absorb.at[:, pl.ds(HALO + x_rows, HALO)],
        absorb.at[:, pl.ds(x_rows, HALO)], absorb.at[:, pl.ds(HALO, HALO)],
    )

    for step in range(slabs + bits):
        if step < slabs:
            opacity(order[step])
            exchange(0, order[step]).start()
        for stage in range(bits):
            at = step - stage - 1
            if not 0 <= at < slabs:
                continue
            slab = order[at]
            exchange(stage, slab).wait_recv()
            if stage < bits - 1:
                half = n >> (stage + 1)
                kept = pl.ds(bases[stage + 1], half)
                acc[slab, kept] = acc[slab, kept] + recvs[stage][slab]
                exchange(stage + 1, slab).start()
            else:
                inner = pl.ds(slab * slab_rows, slab_rows)
                for i in range(per_gas):
                    absorb[i, pl.ds(HALO + slab * slab_rows, slab_rows)] = (
                        KAPPA_FLOOR + strength[me * per_gas + i] * mole[inner]
                        + (acc[slab, position, i] + recvs[stage][slab, 0, i])
                    )
                if at == 1:
                    for copy in absorb_pair:
                        copy.start()

    for copy in pairs + absorb_pair:
        copy.wait()
    absorb[:, 0:HALO] = jnp.where(place == 0, 0.0, absorb[:, 0:HALO])
    absorb[:, HALO + x_rows :] = jnp.where(place == spaces - 1, 0.0, absorb[:, HALO + x_rows :])

    tile = heat.shape[1:]
    y_at = lax.broadcasted_iota(jnp.int32, tile, 0)
    z_at = lax.broadcasted_iota(jnp.int32, tile, 1)
    y_low, y_top = y_at == 0, y_at == tile[0] - 1
    z_low, z_top = z_at == 0, z_at == tile[1] - 1

    def begin(i, row):
        level = heat_w[row]
        square = level * level
        gas = me * per_gas + i
        emitted = (poly[gas, 0] + poly[gas, 1] * level + poly[gas, 2] * square) * (square * square)
        first = absorb[i, row] * emitted
        rem[i, row] = emitted
        res[i, row] = first
        dirs[0, i, row] = first / CENTRE

    for i in range(per_gas):
        begin(i, 0)
        begin(i, rows - 1)

    def face(a, b):
        full = coupling(a + b)
        return full, jnp.where((a > 0.0) & (b > 0.0), full, 0.0)

    lowest = []
    for i in range(per_gas):
        full, off = face(absorb[i, 0], absorb[i, 1])
        cx[i, 1] = off
        lowest.append(full)

    def prepare(row, before):
        following = []
        for i in range(per_gas):
            begin(i, row)
            here = absorb[i, row]
            upper, off = face(here, absorb[i, row + 1])
            cx[i, row + 1] = off
            following.append(upper)
            edge = coupling(here)
            y_face = coupling(here + pltpu.roll(here, 1, 0))
            z_face = coupling(here + pltpu.roll(here, 1, 1))
            cy[i, row] = jnp.where(y_low, 0.0, y_face)
            cz[i, row] = jnp.where(z_low, 0.0, z_face)
            y_up = jnp.where(y_top, edge, pltpu.roll(y_face, tile[0] - 1, 0))
            z_up = jnp.where(z_top, edge, pltpu.roll(z_face, tile[1] - 1, 1))
            diag[i, row] = (
                here + wall_w[row] + before[i] + upper
                + jnp.where(y_low, edge, y_face) + y_up
                + jnp.where(z_low, edge, z_face) + z_up
            )
        return tuple(following)

    lax.fori_loop(1, rows - 1, prepare, tuple(lowest))

    sigma = CENTRE / SPREAD
    ratio = 1.0 / sigma
    for sweep in range(SWEEPS - 1):
        following = 1.0 / (2.0 * sigma - ratio)
        keep, gain = following * ratio, 2.0 * following / SPREAD
        ratio = following
        source, target = sweep % 2, (sweep + 1) % 2

        def relax(row, carry):
            for i in range(per_gas):
                d = dirs[source, i, row]
                c_y, c_z = cy[i, row], cz[i, row]
                applied = diag[i, row] * d
                applied -= cx[i, row] * dirs[source, i, row - 1]
                applied -= cx[i, row + 1] * dirs[source, i, row + 1]
                applied -= c_y * pltpu.roll(d, 1, 0) + pltpu.roll(c_y * d, tile[0] - 1, 0)
                applied -= c_z * pltpu.roll(d, 1, 1) + pltpu.roll(c_z * d, tile[1] - 1, 1)
                left_over = res[i, row] - applied
                res[i, row] = left_over
                rem[i, row] = rem[i, row] - d
                dirs[target, i, row] = keep * d + gain * left_over
            return carry

        lax.fori_loop(1 + sweep, rows - 1 - sweep, relax, 0)

    inner = pl.ds(HALO, x_rows)
    last = (SWEEPS - 1) % 2

    def finish(x, carry):
        row = x + HALO
        total = absorb[0, row] * (rem[0, row] - dirs[last, 0, row])
        for i in range(1, per_gas):
            total += absorb[i, row] * (rem[i, row] - dirs[last, i, row])
        mine[x] = total
        return carry

    lax.fori_loop(0, x_rows, finish, 0)

    chunk = x_rows // n
    own = pl.ds(me * chunk, chunk)
    sends = []
    for k in range(1, n):
        peer = lax.rem(me + k, n)
        sends.append(pltpu.make_async_remote_copy(
            src_ref=mine.at[pl.ds(peer * chunk, chunk)], dst_ref=parts.at[k],
            send_sem=sum_send.at[k], recv_sem=sum_recv.at[k],
            device_id={"gas": peer}, device_id_type=MESH,
        ))
    for copy in sends:
        copy.start()
    total = mine[own]
    for k in range(1, n):
        sends[k - 1].wait_recv()
        total = total + parts[k]
    out[own] = total

    def gather(k, origin):
        held = pl.ds(origin * chunk, chunk)
        return pltpu.make_async_remote_copy(
            src_ref=out.at[held], dst_ref=out.at[held],
            send_sem=gather_send.at[k], recv_sem=gather_recv.at[k],
            device_id={"gas": lax.rem(me + k, n)}, device_id_type=MESH,
        )

    for k in range(1, n):
        gather(k, me).start()
    for k in range(1, n):
        gather(k, lax.rem(me + n - k, n)).wait_recv()

    totals[place] = jnp.sum(out[...], axis=0)

    def share(k, origin):
        return pltpu.make_async_remote_copy(
            src_ref=totals.at[origin], dst_ref=totals.at[origin],
            send_sem=total_send.at[k], recv_sem=total_recv.at[k],
            device_id={"space": lax.rem(place + k, spaces)}, device_id_type=MESH,
        )

    for k in range(1, spaces):
        share(k, place).start()
    for k in range(1, spaces):
        share(k, lax.rem(place + spaces - k, spaces)).wait_recv()
    whole = jnp.sum(jnp.sum(totals[...], axis=0))
    average[0, 0] = whole * (1.0 / (x_rows * spaces * tile[0] * tile[1]))

    for stage in range(bits):
        for slab in range(slabs):
            exchange(stage, slab).wait_send()
    for k in range(1, n):
        sends[k - 1].wait_send()
        gather(k, me).wait_send()
    for k in range(1, spaces):
        share(k, place).wait_send()


def per_device(
    n, spaces, particle_amount, section_opacity, species_opacity_factor,
    absorber_molefraction, scaled_heat_level, wall_touching_flag, fraction_polynomial,
):
    sections, x_rows, ny, nz = particle_amount.shape
    gases = section_opacity.shape[1]
    per_gas = gases // n
    bits = n.bit_length() - 1
    slabs = x_rows // 8
    owners = [reversed_bits(p, bits) for p in range(n)]
    by_place = jnp.concatenate(
        [section_opacity[:, o * per_gas : (o + 1) * per_gas] for o in owners], axis=1
    ).T
    kron = (by_place[:, None, :, None] * jnp.eye(ny, dtype=jnp.bfloat16)[None, :, None, :]).reshape(
        gases * ny, sections * ny
    )
    rows = x_rows + 2 * HALO
    slab_rows = x_rows // slabs
    field = pltpu.VMEM((per_gas, rows, ny, nz), jnp.float32)
    dma = pltpu.SemaphoreType.DMA
    vmem, smem = pl.BlockSpec(memory_space=pltpu.VMEM), pl.BlockSpec(memory_space=pltpu.SMEM)
    divergence, average = pl.pallas_call(
        functools.partial(kernel, n, spaces, slabs, nz),
        out_shape=(
            jax.ShapeDtypeStruct((x_rows, ny, nz), jnp.float32),
            jax.ShapeDtypeStruct((1, 1), jnp.float32),
        ),
        in_specs=[vmem, pl.BlockSpec(memory_space=pl.ANY), smem, vmem, vmem, vmem, smem],
        out_specs=(vmem, smem),
        scratch_shapes=[
            pltpu.VMEM((slabs, sections, slab_rows, ny, nz), jnp.bfloat16),
            pltpu.VMEM((slabs, n, per_gas, slab_rows, ny, nz), jnp.float32),
            [
                pltpu.VMEM((slabs, n >> (stage + 1), per_gas, slab_rows, ny, nz), jnp.float32)
                for stage in range(bits)
            ],
            field,
            pltpu.VMEM((rows, ny, nz), jnp.float32),
            pltpu.VMEM((rows, ny, nz), jnp.float32),
            field, field, field, field, field, field,
            pltpu.VMEM((2, per_gas, rows, ny, nz), jnp.float32),
            pltpu.VMEM((n, x_rows // n, ny, nz), jnp.float32),
            pltpu.VMEM((spaces, ny, nz), jnp.float32),
            pltpu.VMEM((x_rows, ny, nz), jnp.float32),
            dma((slabs,)), dma((bits, slabs)), dma((bits, slabs)), dma((3, 2)), dma((3, 2)),
            dma((n,)), dma((n,)), dma((n,)), dma((n,)), dma((spaces,)), dma((spaces,)),
        ],
        compiler_params=pltpu.CompilerParams(
            collective_id=0, has_side_effects=True, vmem_limit_bytes=56 * 1024 * 1024
        ),
    )(
        kron, particle_amount, species_opacity_factor, absorber_molefraction,
        scaled_heat_level, wall_touching_flag, fraction_polynomial,
    )
    return divergence, average.reshape(())


def solution(mesh):
    return jax.shard_map(
        functools.partial(per_device, mesh.shape["gas"], mesh.shape["space"]),
        mesh=mesh,
        in_specs=(
            P("gas", "space", None, None),
            P("gas", None),
            P(),
            P("space", None, None),
            P("space", None, None),
            P("space", None, None),
            P(),
        ),
        out_specs=(P("space", None, None), P()),
        check_vma=False,
    )
```

time: 325 us -> 139 us (0.43)
  waiting for transfers between devices: 238 us -> 0 us
  Pallas kernels: 0 us -> 123 us
  starting transfers between devices: 29.9 us -> 0 us
  matrix products: 16.8 us -> 0 us
  between operations: 16.2 us -> 2.47 us
  other arithmetic: 11.4 us -> 2.28 us
  blocking collectives: 6.27 us -> 0 us
  local copies, waits for them, and re-layouts: 6.74 us -> 10.9 us
    psum x2 -> x0, waiting for transfers between devices: 228 us -> none  [the longest x1 158 us: per_device(): lax.psum(lax.dot_general(section_opacity, soot_flat, (((0,), (0,)), ((),...]
    pallas_call x0 -> x1, Pallas kernels: none -> 123 us  [per_device(): pl.pallas_call(functools.partial(kernel, n, spaces, slabs, nz), out_shape...]
    ppermute x12 -> x0, starting transfers between devices: 29.8 us -> none  [the longest x6 21.9 us: with_halo(): before = lax.ppermute(last, axis, up)]
    dot_general x1 -> x0, matrix products: 16.8 us -> none  [per_device(): lax.dot_general(section_opacity, soot_flat, (((0,), (0,)), ((), ())), pre...]
    ppermute x12 -> x0, waiting for transfers between devices: 9.08 us -> none  [the longest x6 9.07 us: with_halo(): after = lax.ppermute(leading, axis, down)]
    mul x0 -> x1, local copies, waits for them, and re-layouts: none -> 7.66 us  [per_device(): by_place[:, None, :, None]]
    psum x1 -> x0, blocking collectives: 6.27 us -> none  [per_device(): average_radiative_loss = lax.psum(jnp.sum(divergence), 'space') / cell_count]
    reduce_sum x2 -> x0, other arithmetic: 5.5 us -> none  [the longest x1 3.88 us: per_device(): divergence = lax.psum(jnp.sum(gas_terms, axis=0), 'gas')]
  transfers between devices with their start and end apart: 14 -> 0, of which waited for: 7 -> 0; matrix products, arithmetic and copies ran while one was open for 0% -> 0% of each run, Pallas kernels for 0% -> 0%
where the time goes in v1:
time: 139 us
  Pallas kernels  123 us (88%)
  local copies, waits for them, and re-layouts  10.9 us (8%)
  between operations  2.47 us (2%)
  other arithmetic  2.28 us (2%)
    pallas_call x1, Pallas kernels, per_device(): pl.pallas_call(functools.partial(kernel, n, spaces, slabs, nz), out_shape...  123 us
    mul x1, local copies, waits for them, and re-layouts, per_device(): by_place[:, None, :, None]  7.66 us

profile of v1, /device:TPU:0, one launch (start us, length us, event | category | flops | bytes accessed | tf_op | source)
XLA Modules:
  0.0 139.0 jit_solution(8819681353536852413)
XLA Ops:
  0.6 0.8 fusion.1
  1.5 0.1 concatenate.3
  1.5 0.0 copy-start
  1.6 2.3 %broadcast_multiply_fusion = bf16[16,8,128,8]{3,2,1,0:T(8,128)(2,1)} fusion(bf16[8,8]{1,0:T(8,128)(2,1)S(1)} %fusion, bf16[16,128]{1,0:T(8,128)(2,1)S(1)} %bitcast.4), kind=kLoop, calls=%fused_computation | loop fusion | flops 131072 | bytes 266368 | tf_op jit(solution)/shard_map/mul | solution.py:320
  3.8 7.7 %mul.20.kron = bf16[128,1024]{1,0:T(8,128)(2,1)} reshape(bf16[16,8,128,8]{3,2,1,0:T(8,128)(2,1)} %broadcast_multiply_fusion) | data formatting | bytes 524288 | tf_op jit(solution)/shard_map/mul | solution.py:320
  11.5 0.0 copy-done
  11.5 0.7 copy.10.poly
  12.2 123.3 %shard_map.86 = (f32[64,8,128]{2,1,0:T(8,128)}, f32[1,1]{1,0:T(1,128)}) custom-call(bf16[128,1024]{1,0:T(8,128)(2,1)} %mul.20.kron, bf16[128,64,8,128]{3,2,1,0:T(8,128)(2,1)} %amount.1, f32[16]{0:T(128)} %strength.1, f32[64,8,128]{2,1,0:T(8,128)} %mole.1, f32[64,8,128]{2,1,0:T(8,128)} %heat.1, s32[64,8,128]{2,1,0:T(8,128)} %flag.1, f32[16,3]{1,0:T(8,128)} %copy.10.poly), custom_call_target="tpu_custom_call" | custom-call | tf_op jit(solution)/shard_map/pallas_call | solution.py:328
  135.5 1.7 %copy.13 = f32[64,8,128]{2,1,0:T(8,128)} copy(f32[64,8,128]{2,1,0:T(8,128)} %get-tuple-element.16) | data formatting | bytes 524288
  (1 shorter events, 0.0 us)
Async XLA Ops:
  1.5 10.0 %copy-start = (f32[16,3]{0,1:T(4,128)S(1)}, f32[16,3]{0,1:T(4,128)}, u32[]{:S(2)}) copy-start(f32[16,3]{0,1:T(4,128)} %param.13) | copy-start | bytes 580

commit v2 on v1

--- a/solution.py
+++ b/solution.py
@@ -9,6 +9,7 @@
 
 SWEEPS = 6
 HALO = SWEEPS - 1
+BLOCK = 4
 KAPPA_FLOOR = 0.5
 WALL_LOSS = 0.5
 LAM_LOW = 0.5
@@ -29,10 +30,10 @@
 
 def kernel(
     n, spaces, slabs, cells,
-    kron, amount, strength, mole, heat, flag, poly,
+    opacity_t, amount, strength, mole, heat, flag, poly,
     out, average,
     amount_v, acc, recvs, absorb, heat_w, wall_w, cx, cy, cz, diag, res, rem, dirs,
-    parts, totals, mine,
+    parts, totals, mine, kron,
     load_sem, rs_send, rs_recv, halo_send, halo_recv, sum_send, sum_recv,
     gather_send, gather_recv, total_send, total_recv,
 ):
@@ -62,6 +63,26 @@
         )
     heat_w[HALO : HALO + x_rows] = heat[...]
     wall_w[HALO : HALO + x_rows] = WALL_LOSS * flag[...].astype(jnp.float32)
+    gases, sections = opacity_t.shape
+    ny = heat.shape[1]
+    line = lax.broadcasted_iota(jnp.int32, (gases * ny, gases), 0) // ny
+    wanted = reversed_bits(line // per_gas, bits) * per_gas + line % per_gas
+    picks = wanted == lax.broadcasted_iota(jnp.int32, (gases * ny, gases), 1)
+    spread = lax.broadcasted_iota(jnp.int32, (sections, sections * ny), 1) // ny
+    widens = spread == lax.broadcasted_iota(jnp.int32, (sections, sections * ny), 0)
+    rows_of = jnp.dot(
+        jnp.where(picks, 1.0, 0.0).astype(jnp.bfloat16), opacity_t[...],
+        preferred_element_type=jnp.float32,
+    ).astype(jnp.bfloat16)
+    wide = jnp.dot(
+        rows_of, jnp.where(widens, 1.0, 0.0).astype(jnp.bfloat16),
+        preferred_element_type=jnp.float32,
+    )
+    same = (
+        lax.broadcasted_iota(jnp.int32, wide.shape, 0) % ny
+        == lax.broadcasted_iota(jnp.int32, wide.shape, 1) % ny
+    )
+    kron[...] = jnp.where(same, wide, 0.0).astype(jnp.bfloat16)
     pl.semaphore_wait(barrier, n - 1 + spaces - 1)
 
     right, left = lax.rem(place + 1, spaces), lax.rem(place + spaces - 1, spaces)
@@ -111,8 +132,8 @@
         load(slab).wait()
 
         def one(x, carry):
-            block = amount_v[slab, :, x].reshape(-1, cells)
-            value = jnp.dot(kron[...], block, preferred_element_type=jnp.float32)
+            column = amount_v[slab, :, x].reshape(-1, cells)
+            value = jnp.dot(kron[...], column, preferred_element_type=jnp.float32)
             acc[slab, :, :, x] = value.reshape((n, per_gas) + acc.shape[4:])
             return carry
 
@@ -156,58 +177,61 @@
     absorb[:, HALO + x_rows :] = jnp.where(place == spaces - 1, 0.0, absorb[:, HALO + x_rows :])
 
     tile = heat.shape[1:]
-    y_at = lax.broadcasted_iota(jnp.int32, tile, 0)
-    z_at = lax.broadcasted_iota(jnp.int32, tile, 1)
+    block = (BLOCK,) + tile
+    y_at = lax.broadcasted_iota(jnp.int32, block, 1)
+    z_at = lax.broadcasted_iota(jnp.int32, block, 2)
     y_low, y_top = y_at == 0, y_at == tile[0] - 1
     z_low, z_top = z_at == 0, z_at == tile[1] - 1
 
-    def begin(i, row):
-        level = heat_w[row]
+    def begin(i, at):
+        level = heat_w[at]
         square = level * level
         gas = me * per_gas + i
-        emitted = (poly[gas, 0] + poly[gas, 1] * level + poly[gas, 2] * square) * (square * square)
-        first = absorb[i, row] * emitted
-        rem[i, row] = emitted
-        res[i, row] = first
-        dirs[0, i, row] = first / CENTRE
-
-    for i in range(per_gas):
-        begin(i, 0)
-        begin(i, rows - 1)
+        emitted = (poly[0, gas] + poly[1, gas] * level + poly[2, gas] * square) * (square * square)
+        first = absorb[i, at] * emitted
+        return emitted, first, first / CENTRE
+
+    def put_begin(i, at, values):
+        rem[i, at], res[i, at], dirs[0, i, at] = values
 
     def face(a, b):
         full = coupling(a + b)
         return full, jnp.where((a > 0.0) & (b > 0.0), full, 0.0)
 
-    lowest = []
     for i in range(per_gas):
-        full, off = face(absorb[i, 0], absorb[i, 1])
-        cx[i, 1] = off
-        lowest.append(full)
-
-    def prepare(row, before):
-        following = []
+        for at in (pl.ds(0, 1), pl.ds(rows - 1, 1)):
+            put_begin(i, at, begin(i, at))
+            dirs[1, i, at] = jnp.zeros((1,) + tile, jnp.float32)
+        cx[i, rows - 1] = face(absorb[i, rows - 2], absorb[i, rows - 1])[1]
+
+    def prepare(step, carry):
+        row = 1 + step * BLOCK
+        at = pl.ds(row, BLOCK)
+        found = []
         for i in range(per_gas):
-            begin(i, row)
-            here = absorb[i, row]
-            upper, off = face(here, absorb[i, row + 1])
-            cx[i, row + 1] = off
-            following.append(upper)
+            around = absorb[i, pl.ds(row - 1, BLOCK + 2)]
+            here = around[1:-1]
+            full, off = face(around[:-1], around[1:])
             edge = coupling(here)
-            y_face = coupling(here + pltpu.roll(here, 1, 0))
-            z_face = coupling(here + pltpu.roll(here, 1, 1))
-            cy[i, row] = jnp.where(y_low, 0.0, y_face)
-            cz[i, row] = jnp.where(z_low, 0.0, z_face)
-            y_up = jnp.where(y_top, edge, pltpu.roll(y_face, tile[0] - 1, 0))
-            z_up = jnp.where(z_top, edge, pltpu.roll(z_face, tile[1] - 1, 1))
-            diag[i, row] = (
-                here + wall_w[row] + before[i] + upper
+            y_face = coupling(here + pltpu.roll(here, 1, 1))
+            z_face = coupling(here + pltpu.roll(here, 1, 2))
+            y_up = jnp.where(y_top, edge, pltpu.roll(y_face, tile[0] - 1, 1))
+            z_up = jnp.where(z_top, edge, pltpu.roll(z_face, tile[1] - 1, 2))
+            middle = (
+                here + wall_w[at] + full[:-1] + full[1:]
                 + jnp.where(y_low, edge, y_face) + y_up
                 + jnp.where(z_low, edge, z_face) + z_up
             )
-        return tuple(following)
-
-    lax.fori_loop(1, rows - 1, prepare, tuple(lowest))
+            found.append((
+                off[:-1], jnp.where(y_low, 0.0, y_face), jnp.where(z_low, 0.0, z_face), middle,
+                begin(i, at),
+            ))
+        for i in range(per_gas):
+            cx[i, at], cy[i, at], cz[i, at], diag[i, at], values = found[i]
+            put_begin(i, at, values)
+        return carry
+
+    lax.fori_loop(0, (rows - 2) // BLOCK, prepare, 0)
 
     sigma = CENTRE / SPREAD
     ratio = 1.0 / sigma
@@ -216,36 +240,40 @@
         keep, gain = following * ratio, 2.0 * following / SPREAD
         ratio = following
         source, target = sweep % 2, (sweep + 1) % 2
-
-        def relax(row, carry):
+        skip = sweep * 2 // BLOCK * BLOCK // 2
+
+        def relax(step, carry):
+            row = 1 + skip + step * BLOCK
+            at = pl.ds(row, BLOCK)
+            found = []
             for i in range(per_gas):
-                d = dirs[source, i, row]
-                c_y, c_z = cy[i, row], cz[i, row]
-                applied = diag[i, row] * d
-                applied -= cx[i, row] * dirs[source, i, row - 1]
-                applied -= cx[i, row + 1] * dirs[source, i, row + 1]
-                applied -= c_y * pltpu.roll(d, 1, 0) + pltpu.roll(c_y * d, tile[0] - 1, 0)
-                applied -= c_z * pltpu.roll(d, 1, 1) + pltpu.roll(c_z * d, tile[1] - 1, 1)
-                left_over = res[i, row] - applied
-                res[i, row] = left_over
-                rem[i, row] = rem[i, row] - d
-                dirs[target, i, row] = keep * d + gain * left_over
+                around = dirs[source, i, pl.ds(row - 1, BLOCK + 2)]
+                d = around[1:-1]
+                c_x, c_y, c_z = cx[i, pl.ds(row, BLOCK + 1)], cy[i, at], cz[i, at]
+                applied = diag[i, at] * d
+                applied -= c_x[:-1] * around[:-2]
+                applied -= c_x[1:] * around[2:]
+                applied -= c_y * pltpu.roll(d, 1, 1) + pltpu.roll(c_y * d, tile[0] - 1, 1)
+                applied -= c_z * pltpu.roll(d, 1, 2) + pltpu.roll(c_z * d, tile[1] - 1, 2)
+                left_over = res[i, at] - applied
+                found.append((left_over, rem[i, at] - d, keep * d + gain * left_over))
+            for i in range(per_gas):
+                res[i, at], rem[i, at], dirs[target, i, at] = found[i]
             return carry
 
-        lax.fori_loop(1 + sweep, rows - 1 - sweep, relax, 0)
-
-    inner = pl.ds(HALO, x_rows)
+        lax.fori_loop(0, (rows - 2 - 2 * skip) // BLOCK, relax, 0)
+
     last = (SWEEPS - 1) % 2
 
-    def finish(x, carry):
-        row = x + HALO
-        total = absorb[0, row] * (rem[0, row] - dirs[last, 0, row])
+    def finish(step, carry):
+        at = pl.ds(HALO + step * BLOCK, BLOCK)
+        total = absorb[0, at] * (rem[0, at] - dirs[last, 0, at])
         for i in range(1, per_gas):
-            total += absorb[i, row] * (rem[i, row] - dirs[last, i, row])
-        mine[x] = total
+            total += absorb[i, at] * (rem[i, at] - dirs[last, i, at])
+        mine[pl.ds(step * BLOCK, BLOCK)] = total
         return carry
 
-    lax.fori_loop(0, x_rows, finish, 0)
+    lax.fori_loop(0, x_rows // BLOCK, finish, 0)
 
     chunk = x_rows // n
     own = pl.ds(me * chunk, chunk)
@@ -313,13 +341,6 @@
     per_gas = gases // n
     bits = n.bit_length() - 1
     slabs = x_rows // 8
-    owners = [reversed_bits(p, bits) for p in range(n)]
-    by_place = jnp.concatenate(
-        [section_opacity[:, o * per_gas : (o + 1) * per_gas] for o in owners], axis=1
-    ).T
-    kron = (by_place[:, None, :, None] * jnp.eye(ny, dtype=jnp.bfloat16)[None, :, None, :]).reshape(
-        gases * ny, sections * ny
-    )
     rows = x_rows + 2 * HALO
     slab_rows = x_rows // slabs
     field = pltpu.VMEM((per_gas, rows, ny, nz), jnp.float32)
@@ -348,6 +369,7 @@
             pltpu.VMEM((n, x_rows // n, ny, nz), jnp.float32),
             pltpu.VMEM((spaces, ny, nz), jnp.float32),
             pltpu.VMEM((x_rows, ny, nz), jnp.float32),
+            pltpu.VMEM((gases * ny, sections * ny), jnp.bfloat16),
             dma((slabs,)), dma((bits, slabs)), dma((bits, slabs)), dma((3, 2)), dma((3, 2)),
             dma((n,)), dma((n,)), dma((n,)), dma((n,)), dma((spaces,)), dma((spaces,)),
         ],
@@ -355,8 +377,8 @@
             collective_id=0, has_side_effects=True, vmem_limit_bytes=56 * 1024 * 1024
         ),
     )(
-        kron, particle_amount, species_opacity_factor, absorber_molefraction,
-        scaled_heat_level, wall_touching_flag, fraction_polynomial,
+        section_opacity.T, particle_amount, species_opacity_factor, absorber_molefraction,
+        scaled_heat_level, wall_touching_flag, fraction_polynomial.T,
     )
     return divergence, average.reshape(())
 

time: 139 us -> 97.2 us (0.70)
  Pallas kernels: 123 us -> 93 us
  local copies, waits for them, and re-layouts: 10.9 us -> 1.67 us
  other arithmetic: 2.28 us -> 0 us
    pallas_call x1, Pallas kernels: 123 us -> 93 us  [per_device(): pl.pallas_call(functools.partial(kernel, n, spaces, slabs, nz), out_shape...]
    mul x1 -> x0, local copies, waits for them, and re-layouts: 7.66 us -> none  [per_device(): by_place[:, None, :, None]]
    mul x1 -> x0, other arithmetic: 2.28 us -> none  [per_device(): by_place[:, None, :, None]]
where the time goes in v2:
time: 97.2 us; the launch traced here: 97.1 us
  Pallas kernels  93 us (96%)
  between operations  2.41 us (2%)
  local copies, waits for them, and re-layouts  1.67 us (2%)
    pallas_call x1, Pallas kernels, per_device(): pl.pallas_call(functools.partial(kernel, n, spaces, slabs, nz), out_shape...  93 us

profile of v2, /device:TPU:0, one launch (start us, length us, event | category | flops | bytes accessed | tf_op | source)
XLA Modules:
  0.0 97.1 jit_solution(796132059202369197)
XLA Ops:
  0.6 93.0 %shard_map.86 = (f32[64,8,128]{2,1,0:T(8,128)}, f32[1,1]{1,0:T(1,128)}) custom-call(bf16[16,128]{1,0:T(8,128)(2,1)} %bitcast.3, bf16[128,64,8,128]{3,2,1,0:T(8,128)(2,1)} %amount.1, f32[16]{0:T(128)} %strength.1, f32[64,8,128]{2,1,0:T(8,128)} %mole.1, f32[64,8,128]{2,1,0:T(8,128)} %heat.1, s32[64,8,128]{2,1,0:T(8,128)} %flag.1, f32[3,16]{1,0:T(4,128)} %bitcast.4), custom_call_target="tpu_custom_call" | custom-call | tf_op jit(solution)/shard_map/pallas_call | solution.py:349
  93.6 1.7 %copy.11 = f32[64,8,128]{2,1,0:T(8,128)} copy(f32[64,8,128]{2,1,0:T(8,128)} %get-tuple-element.8) | data formatting | bytes 524288

commit v3 on v2

--- a/solution.py
+++ b/solution.py
@@ -10,6 +10,9 @@
 SWEEPS = 6
 HALO = SWEEPS - 1
 BLOCK = 4
+AHEAD = 3
+SLAB_ROWS = 8
+Z_FIRST = (1,)
 KAPPA_FLOOR = 0.5
 WALL_LOSS = 0.5
 LAM_LOW = 0.5
@@ -19,10 +22,6 @@
 MESH = pl.DeviceIdType.MESH
 
 
-def reversed_bits(index, bits):
-    return sum(((index >> b) & 1) << (bits - 1 - b) for b in range(bits))
-
-
 def coupling(total):
     positive = total > 0.0
     return jnp.where(positive, 2.0 / (3.0 * jnp.where(positive, total, 1.0)), 0.0)
@@ -33,23 +32,31 @@
     opacity_t, amount, strength, mole, heat, flag, poly,
     out, average,
     amount_v, acc, recvs, absorb, heat_w, wall_w, cx, cy, cz, diag, res, rem, dirs,
-    parts, totals, mine, kron,
+    parts, totals, gas_totals, mine, kron,
     load_sem, rs_send, rs_recv, halo_send, halo_recv, sum_send, sum_recv,
-    gather_send, gather_recv, total_send, total_recv,
+    gather_send, gather_recv, total_send, total_recv, greet_send, greet_recv,
 ):
     bits = n.bit_length() - 1
     me, place = lax.axis_index("gas"), lax.axis_index("space")
     per_gas = acc.shape[2]
     x_rows, rows = heat.shape[0], heat_w.shape[0]
     slab_rows = x_rows // slabs
-    order = [0, slabs - 1] + list(range(1, slabs - 1))
+    edge = -(-HALO // slab_rows)
+    order = (
+        list(range(edge)) + list(range(slabs - edge, slabs)) + list(range(edge, slabs - edge))
+    )
+    low_first = list(range(bits))
+    high_first = low_first[1:] + low_first[:1]
+    bit_order = {
+        slab: high_first if at % 8 in Z_FIRST else low_first for at, slab in enumerate(order)
+    }
 
     def load(slab):
         return pltpu.make_async_copy(
             amount.at[:, pl.ds(slab * slab_rows, slab_rows)], amount_v.at[slab], load_sem.at[slab]
         )
 
-    for slab in order:
+    for slab in order[:AHEAD]:
         load(slab).start()
 
     barrier = pltpu.get_barrier_semaphore()
@@ -66,8 +73,7 @@
     gases, sections = opacity_t.shape
     ny = heat.shape[1]
     line = lax.broadcasted_iota(jnp.int32, (gases * ny, gases), 0) // ny
-    wanted = reversed_bits(line // per_gas, bits) * per_gas + line % per_gas
-    picks = wanted == lax.broadcasted_iota(jnp.int32, (gases * ny, gases), 1)
+    picks = line == lax.broadcasted_iota(jnp.int32, (gases * ny, gases), 1)
     spread = lax.broadcasted_iota(jnp.int32, (sections, sections * ny), 1) // ny
     widens = spread == lax.broadcasted_iota(jnp.int32, (sections, sections * ny), 0)
     rows_of = jnp.dot(
@@ -111,18 +117,23 @@
     for copy in pairs:
         copy.start()
 
-    bases, size = [jnp.int32(0)], n
-    for stage in range(bits):
-        size //= 2
-        bases.append(bases[-1] + ((me >> stage) & 1) * size)
-    position = bases[bits]
+    def base(stage, slab):
+        return sum(
+            ((me >> bit) & 1) * (n >> (at + 1)) for at, bit in enumerate(bit_order[slab][:stage])
+        ) + jnp.int32(0)
+
+    def spot(owner, slab):
+        return sum(
+            ((owner >> bit) & 1) * (n >> (at + 1)) for at, bit in enumerate(bit_order[slab])
+        )
 
     def exchange(stage, slab):
         half = n >> (stage + 1)
-        bit = (me >> stage) & 1
-        partner = me + (1 - 2 * bit) * (1 << stage)
+        level = bit_order[slab][stage]
+        bit = (me >> level) & 1
+        partner = me + (1 - 2 * bit) * (1 << level)
         return pltpu.make_async_remote_copy(
-            src_ref=acc.at[slab, pl.ds(bases[stage] + (1 - bit) * half, half)],
+            src_ref=acc.at[slab, pl.ds(base(stage, slab) + (1 - bit) * half, half)],
             dst_ref=recvs[stage].at[slab],
             send_sem=rs_send.at[stage, slab], recv_sem=rs_recv.at[stage, slab],
             device_id={"gas": partner}, device_id_type=MESH,
@@ -134,7 +145,9 @@
         def one(x, carry):
             column = amount_v[slab, :, x].reshape(-1, cells)
             value = jnp.dot(kron[...], column, preferred_element_type=jnp.float32)
-            acc[slab, :, :, x] = value.reshape((n, per_gas) + acc.shape[4:])
+            value = value.reshape((n, per_gas) + acc.shape[4:])
+            for owner in range(n):
+                acc[slab, spot(owner, slab), :, x] = value[owner]
             return carry
 
         lax.fori_loop(0, slab_rows, one, 0)
@@ -147,6 +160,8 @@
 
     for step in range(slabs + bits):
         if step < slabs:
+            if step + AHEAD < slabs:
+                load(order[step + AHEAD]).start()
             opacity(order[step])
             exchange(0, order[step]).start()
         for stage in range(bits):
@@ -157,7 +172,7 @@
             exchange(stage, slab).wait_recv()
             if stage < bits - 1:
                 half = n >> (stage + 1)
-                kept = pl.ds(bases[stage + 1], half)
+                kept = pl.ds(base(stage + 1, slab), half)
                 acc[slab, kept] = acc[slab, kept] + recvs[stage][slab]
                 exchange(stage + 1, slab).start()
             else:
@@ -165,9 +180,9 @@
                 for i in range(per_gas):
                     absorb[i, pl.ds(HALO + slab * slab_rows, slab_rows)] = (
                         KAPPA_FLOOR + strength[me * per_gas + i] * mole[inner]
-                        + (acc[slab, position, i] + recvs[stage][slab, 0, i])
+                        + (acc[slab, base(bits, slab), i] + recvs[stage][slab, 0, i])
                     )
-                if at == 1:
+                if at == 2 * edge - 1:
                     for copy in absorb_pair:
                         copy.start()
 
@@ -271,9 +286,11 @@
         for i in range(1, per_gas):
             total += absorb[i, at] * (rem[i, at] - dirs[last, i, at])
         mine[pl.ds(step * BLOCK, BLOCK)] = total
-        return carry
-
-    lax.fori_loop(0, x_rows // BLOCK, finish, 0)
+        return carry + jnp.sum(total, axis=0)
+
+    gas_totals[me] = lax.fori_loop(
+        0, x_rows // BLOCK, finish, jnp.zeros(tile, jnp.float32)
+    )
 
     chunk = x_rows // n
     own = pl.ds(me * chunk, chunk)
@@ -285,6 +302,15 @@
             send_sem=sum_send.at[k], recv_sem=sum_recv.at[k],
             device_id={"gas": peer}, device_id_type=MESH,
         ))
+    def greet(k, origin):
+        return pltpu.make_async_remote_copy(
+            src_ref=gas_totals.at[origin], dst_ref=gas_totals.at[origin],
+            send_sem=greet_send.at[k], recv_sem=greet_recv.at[k],
+            device_id={"gas": lax.rem(me + k, n)}, device_id_type=MESH,
+        )
+
+    for k in range(1, n):
+        greet(k, me).start()
     for copy in sends:
         copy.start()
     total = mine[own]
@@ -304,9 +330,8 @@
     for k in range(1, n):
         gather(k, me).start()
     for k in range(1, n):
-        gather(k, lax.rem(me + n - k, n)).wait_recv()
-
-    totals[place] = jnp.sum(out[...], axis=0)
+        greet(k, lax.rem(me + n - k, n)).wait_recv()
+    totals[place] = jnp.sum(gas_totals[...], axis=0)
 
     def share(k, origin):
         return pltpu.make_async_remote_copy(
@@ -319,6 +344,8 @@
         share(k, place).start()
     for k in range(1, spaces):
         share(k, lax.rem(place + spaces - k, spaces)).wait_recv()
+    for k in range(1, n):
+        gather(k, lax.rem(me + n - k, n)).wait_recv()
     whole = jnp.sum(jnp.sum(totals[...], axis=0))
     average[0, 0] = whole * (1.0 / (x_rows * spaces * tile[0] * tile[1]))
 
@@ -328,6 +355,7 @@
     for k in range(1, n):
         sends[k - 1].wait_send()
         gather(k, me).wait_send()
+        greet(k, me).wait_send()
     for k in range(1, spaces):
         share(k, place).wait_send()
 
@@ -340,7 +368,7 @@
     gases = section_opacity.shape[1]
     per_gas = gases // n
     bits = n.bit_length() - 1
-    slabs = x_rows // 8
+    slabs = x_rows // SLAB_ROWS
     rows = x_rows + 2 * HALO
     slab_rows = x_rows // slabs
     field = pltpu.VMEM((per_gas, rows, ny, nz), jnp.float32)
@@ -368,10 +396,12 @@
             pltpu.VMEM((2, per_gas, rows, ny, nz), jnp.float32),
             pltpu.VMEM((n, x_rows // n, ny, nz), jnp.float32),
             pltpu.VMEM((spaces, ny, nz), jnp.float32),
+            pltpu.VMEM((n, ny, nz), jnp.float32),
             pltpu.VMEM((x_rows, ny, nz), jnp.float32),
             pltpu.VMEM((gases * ny, sections * ny), jnp.bfloat16),
             dma((slabs,)), dma((bits, slabs)), dma((bits, slabs)), dma((3, 2)), dma((3, 2)),
             dma((n,)), dma((n,)), dma((n,)), dma((n,)), dma((spaces,)), dma((spaces,)),
+            dma((n,)), dma((n,)),
         ],
         compiler_params=pltpu.CompilerParams(
             collective_id=0, has_side_effects=True, vmem_limit_bytes=56 * 1024 * 1024

time: 97.2 us -> 94 us (0.967)
  Pallas kernels: 93 us -> 89.8 us
    pallas_call x1, Pallas kernels: 93 us -> 89.8 us  [per_device(): pl.pallas_call(functools.partial(kernel, n, spaces, slabs, nz), out_shape...]
where the time goes in v3:
time: 94 us; the launch traced here: 93.8 us
  Pallas kernels  89.8 us (96%)
  between operations  2.41 us (3%)
  local copies, waits for them, and re-layouts  1.67 us (2%)
    pallas_call x1, Pallas kernels, per_device(): pl.pallas_call(functools.partial(kernel, n, spaces, slabs, nz), out_shape...  89.8 us

profile of v3, /device:TPU:0, one launch (start us, length us, event | category | flops | bytes accessed | tf_op | source)
XLA Modules:
  0.0 93.8 jit_solution(4772487903190871150)
XLA Ops:
  0.6 89.8 %shard_map.86 = (f32[64,8,128]{2,1,0:T(8,128)}, f32[1,1]{1,0:T(1,128)}) custom-call(bf16[16,128]{1,0:T(8,128)(2,1)} %bitcast.3, bf16[128,64,8,128]{3,2,1,0:T(8,128)(2,1)} %amount.1, f32[16]{0:T(128)} %strength.1, f32[64,8,128]{2,1,0:T(8,128)} %mole.1, f32[64,8,128]{2,1,0:T(8,128)} %heat.1, s32[64,8,128]{2,1,0:T(8,128)} %flag.1, f32[3,16]{1,0:T(4,128)} %bitcast.4), custom_call_target="tpu_custom_call" | custom-call | tf_op jit(solution)/shard_map/pallas_call | solution.py:377
  90.4 1.7 %copy.11 = f32[64,8,128]{2,1,0:T(8,128)} copy(f32[64,8,128]{2,1,0:T(8,128)} %get-tuple-element.8) | data formatting | bytes 524288

commit v4 on v3

--- a/solution.py
+++ b/solution.py
@@ -9,7 +9,7 @@
 
 SWEEPS = 6
 HALO = SWEEPS - 1
-BLOCK = 4
+BLOCK = 8
 AHEAD = 3
 SLAB_ROWS = 8
 Z_FIRST = (1,)

time: 94 us -> 89.7 us (0.954)
  Pallas kernels: 89.8 us -> 85.4 us
    pallas_call x1, Pallas kernels: 89.8 us -> 85.4 us  [per_device(): pl.pallas_call(functools.partial(kernel, n, spaces, slabs, nz), out_shape...]
where the time goes in v4:
time: 89.7 us; the launch traced here: 89.5 us
  Pallas kernels  85.4 us (95%)
  between operations  2.41 us (3%)
  local copies, waits for them, and re-layouts  1.67 us (2%)
    pallas_call x1, Pallas kernels, per_device(): pl.pallas_call(functools.partial(kernel, n, spaces, slabs, nz), out_shape...  85.4 us

profile of v4, /device:TPU:0, one launch (start us, length us, event | category | flops | bytes accessed | tf_op | source)
XLA Modules:
  0.0 89.5 jit_solution(188463452517556947)
XLA Ops:
  0.6 85.4 %shard_map.86 = (f32[64,8,128]{2,1,0:T(8,128)}, f32[1,1]{1,0:T(1,128)}) custom-call(bf16[16,128]{1,0:T(8,128)(2,1)} %bitcast.3, bf16[128,64,8,128]{3,2,1,0:T(8,128)(2,1)} %amount.1, f32[16]{0:T(128)} %strength.1, f32[64,8,128]{2,1,0:T(8,128)} %mole.1, f32[64,8,128]{2,1,0:T(8,128)} %heat.1, s32[64,8,128]{2,1,0:T(8,128)} %flag.1, f32[3,16]{1,0:T(4,128)} %bitcast.4), custom_call_target="tpu_custom_call" | custom-call | tf_op jit(solution)/shard_map/pallas_call | solution.py:377
  86.0 1.7 %copy.11 = f32[64,8,128]{2,1,0:T(8,128)} copy(f32[64,8,128]{2,1,0:T(8,128)} %get-tuple-element.8) | data formatting | bytes 524288

commit v5 on v4

--- a/solution.py
+++ b/solution.py
@@ -164,7 +164,7 @@
                 load(order[step + AHEAD]).start()
             opacity(order[step])
             exchange(0, order[step]).start()
-        for stage in range(bits):
+        for stage in reversed(range(bits)):
             at = step - stage - 1
             if not 0 <= at < slabs:
                 continue

time: 89.7 us -> 91.6 us (1.021)
  Pallas kernels: 85.4 us -> 87.4 us
    pallas_call x1, Pallas kernels: 85.4 us -> 87.4 us  [per_device(): pl.pallas_call(functools.partial(kernel, n, spaces, slabs, nz), out_shape...]
where the time goes in v5:
time: 91.6 us; the launch traced here: 91.5 us
  Pallas kernels  87.4 us (95%)
  between operations  2.41 us (3%)
  local copies, waits for them, and re-layouts  1.67 us (2%)
    pallas_call x1, Pallas kernels, per_device(): pl.pallas_call(functools.partial(kernel, n, spaces, slabs, nz), out_shape...  87.4 us

profile of v5, /device:TPU:0, one launch (start us, length us, event | category | flops | bytes accessed | tf_op | source)
XLA Modules:
  0.0 91.5 jit_solution(12597461655704020310)
XLA Ops:
  0.6 87.4 %shard_map.86 = (f32[64,8,128]{2,1,0:T(8,128)}, f32[1,1]{1,0:T(1,128)}) custom-call(bf16[16,128]{1,0:T(8,128)(2,1)} %bitcast.3, bf16[128,64,8,128]{3,2,1,0:T(8,128)(2,1)} %amount.1, f32[16]{0:T(128)} %strength.1, f32[64,8,128]{2,1,0:T(8,128)} %mole.1, f32[64,8,128]{2,1,0:T(8,128)} %heat.1, s32[64,8,128]{2,1,0:T(8,128)} %flag.1, f32[3,16]{1,0:T(4,128)} %bitcast.4), custom_call_target="tpu_custom_call" | custom-call | tf_op jit(solution)/shard_map/pallas_call | solution.py:377
  88.0 1.7 %copy.11 = f32[64,8,128]{2,1,0:T(8,128)} copy(f32[64,8,128]{2,1,0:T(8,128)} %get-tuple-element.8) | data formatting | bytes 524288
